TPU v7x, 256 devices: a whole 4x4x8 slice. The times are simulated.
256 devices in a mesh: group: 32 (over y, x, core), tensor: 8 (over z).
Axes of the slice: x: 4, y: 4, z: 8, core: 2. Of those that a mesh axis runs over, the one named last changes fastest.
Arguments:
- hidden: bfloat16 [32, 2, 256, 4096], P('group', None, 'tensor'), may hold values from -6 to 6
- norm_gain: bfloat16 [4096], replicated, may hold values from 0.5 to 1.5
- w_query: bfloat16 [4096, 4096], P(None, 'tensor'), may hold values from -0.09375 to 0.09375
- w_key: bfloat16 [4096, 1024], P(None, 'tensor'), may hold values from -0.09375 to 0.09375
- w_value: bfloat16 [4096, 1024], P(None, 'tensor'), may hold values from -0.09375 to 0.09375
- w_output: bfloat16 [4096, 4096], P('tensor'), may hold values from -0.09375 to 0.09375
- prefix_pool: bfloat16 [65536, 8, 2048], P('group', None, 'tensor'), may hold values from -120 to 120
- page_table: int32 [32, 2, 1024], P('group'), may hold values from 0 to 1023, each once within a row
- prefix_len: int32 [32, 2], replicated, may hold values from 1024 to 8192
- source: int32 [32], replicated, may hold values from 0 to 31, as said below
- decode_owner: int32 [32, 32], replicated, may hold values from 0 to 31, as said below
Outputs:
- layer_out: bfloat16 [8192, 4096], P(('group', 'tensor'))
- decode_pool: bfloat16 [1024, 8, 2048], P('group', None, 'tensor')
Inputs may be any that keep to these rules, and one draw needn't show every extreme that they name: source[h] is h or h - 1 modulo 32. For each page index k, the values decode_owner[h, k] over all h are all different; no row names one group more than 2 times, and some row names a group exactly 2 times.
All inputs are finite; a program needn't handle non-finite values.
Results may differ from a plain program's by a relative error of at most 0.012.
Values may be sent and summed in bfloat16 or wider, within the bound.
No kernel may reach another device: no remote copies, remote signals or barrier semaphores. Data moves between devices by JAX's collectives and lax.ppermute only.
A program may use at most 128 MiB of HBM per device.

v0:
```python
import math

import jax
import jax.numpy as jnp
from jax import lax
from jax.sharding import PartitionSpec as P

HD = 128
PAGE = 8
BLOCK = 256
PREFIX = 8192


EPS = 1e-05
THETA = 500000.0


def from_behind(block, axis, distance):
    devices = range(lax.axis_size(axis))
    route = [((i - distance) % len(devices), i) for i in devices]
    return lax.ppermute(block, axis, route)


def rotate(values, positions):
    half_dim = values.shape[-1] // 2
    frequency = THETA ** (-(jnp.arange(half_dim, dtype=jnp.float32) * 2.0) / values.shape[-1])
    angles = positions[..., None] * frequency
    cosine = jnp.cos(angles)[..., None, :]
    sines = jnp.sin(angles)[..., None, :]
    first_half = values[..., :half_dim]
    second = values[..., half_dim:]
    return jnp.concatenate(
        [first_half * cosine - second * sines, second * cosine + first_half * sines], axis=-1
    )


def choose(flag, taken_part, own_part):
    return jax.tree.map(
        lambda taken, current: jnp.where(flag, taken, current), taken_part, own_part
    )


def attend(grouped, all_keys, all_values, allowed, score_scale):
    scores = (
        jnp.einsum("qhgd,khd->hgqk", grouped, all_keys, preferred_element_type=jnp.float32)
        * score_scale
    )
    scores = jnp.where(allowed, scores, -jnp.inf)
    row_max = jnp.max(scores, axis=-1)
    exp_scores = jnp.exp(scores - row_max[..., None])
    row_total = jnp.sum(exp_scores, axis=-1)
    weighted = jnp.einsum(
        "hgqk,khd->qhgd",
        exp_scores.astype(jnp.bfloat16),
        all_values,
        preferred_element_type=jnp.float32,
    )
    return (weighted, row_max, row_total)


def to_rows(factor):
    return jnp.transpose(factor, (2, 0, 1))[..., None]


def full_attention(grouped, new_keys, new_values, prefix_kv, prefix_count):
    kv_heads = new_keys.shape[1]
    block_len = new_keys.shape[0]
    prefix_split = prefix_kv.reshape(PREFIX, kv_heads, 2, HD)
    all_keys = jnp.concatenate([prefix_split[:, :, 0], new_keys], axis=0)
    all_values = jnp.concatenate([prefix_split[:, :, 1], new_values], axis=0)
    column = jnp.arange(PREFIX + block_len)[None, :]
    row_index = jnp.arange(block_len)[:, None]
    allowed = jnp.where(column < PREFIX, column < prefix_count, column - PREFIX <= row_index)
    weighted, row_max, row_total = attend(
        grouped, all_keys, all_values, allowed, 1.0 / math.sqrt(HD)
    )
    return (weighted / to_rows(row_total)).astype(jnp.bfloat16)


def local(
    hidden,
    norm_gain,
    w_query,
    w_key,
    w_value,
    w_output,
    prefix_pool,
    page_table,
    prefix_len,
    source,
    decode_owner,
):
    groups = lax.axis_size("group")
    my_group = lax.axis_index("group")
    query_width = w_query.shape[1]
    key_width = w_key.shape[1]
    query_heads = query_width // HD
    kv_heads = key_width // HD
    group_size = query_heads // kv_heads
    kv_cols = prefix_pool.shape[2]
    region = prefix_pool.shape[0] // 2
    lower_group = (my_group + groups - 1) % groups
    take_lower = source[my_group] == lower_group
    own_counts = prefix_len[my_group]
    prefix_count = jnp.where(take_lower, prefix_len[lower_group, 1], own_counts[0])
    ordered_first = jnp.take(prefix_pool, page_table[0, 0], axis=0).reshape(PREFIX, kv_cols)
    ordered_second = jnp.take(prefix_pool, region + page_table[0, 1], axis=0).reshape(
        PREFIX, kv_cols
    )
    handed_pair = from_behind((hidden[0, 1], ordered_second), "group", 1)
    chosen_rows, prefix_kv = choose(take_lower, handed_pair, (hidden[0, 0], ordered_first))
    block_rows = chosen_rows[None]
    counts = prefix_count[None]
    block_f32 = block_rows.astype(jnp.float32)
    mean_square = jnp.mean(block_f32 * block_f32, axis=-1, keepdims=True)
    normed = (block_f32 * lax.rsqrt(mean_square + EPS) * norm_gain.astype(jnp.float32)).astype(
        jnp.bfloat16
    )
    piece = lax.all_gather(normed, "tensor", axis=1, tiled=True)
    flat = piece.reshape(-1, piece.shape[-1])
    joined = jnp.concatenate(
        [
            jnp.dot(flat, w_query, preferred_element_type=jnp.float32),
            jnp.dot(flat, w_key, preferred_element_type=jnp.float32),
            jnp.dot(flat, w_value, preferred_element_type=jnp.float32),
        ],
        axis=1,
    )
    projected = joined.reshape(piece.shape[0], piece.shape[1], joined.shape[1])
    slots = projected.shape[0]
    block_len = projected.shape[1]
    positions = (counts[:, None] + jnp.arange(block_len, dtype=jnp.int32)[None, :]).astype(
        jnp.float32
    )
    queries = rotate(
        projected[..., :query_width].reshape(slots, block_len, query_heads, HD), positions
    ).astype(jnp.bfloat16)
    new_keys = rotate(
        projected[..., query_width : query_width + key_width].reshape(
            slots, block_len, kv_heads, HD
        ),
        positions,
    ).astype(jnp.bfloat16)
    new_values = (
        projected[..., query_width + key_width :]
        .reshape(slots, block_len, kv_heads, HD)
        .astype(jnp.bfloat16)
    )
    grouped = queries.reshape(slots, block_len, kv_heads, group_size, HD)
    attended = jax.vmap(full_attention)(grouped, new_keys, new_values, prefix_kv[None], counts)
    by_rows = jnp.transpose(attended.reshape(slots, block_len, query_width), (1, 0, 2))
    summed = lax.psum_scatter(
        jnp.einsum("bsc,cd->bsd", by_rows, w_output, preferred_element_type=jnp.float32).astype(
            jnp.bfloat16
        ),
        "tensor",
        scatter_dimension=0,
        tiled=True,
    ).astype(jnp.float32)
    layer_rows = (block_f32 + jnp.transpose(summed, (1, 0, 2))).astype(jnp.bfloat16)
    new_cache = jnp.stack([new_keys, new_values], axis=3).reshape(slots, block_len, kv_cols)
    layer_out = layer_rows[0]
    new_kv = new_cache[0]
    page_count = BLOCK // PAGE
    spread_count = min(groups, page_count - page_count // 4)
    slot_cap = (page_count + spread_count - 1) // spread_count
    page_ids = jnp.arange(page_count)
    earlier = page_ids[None, :] < page_ids[:, None]
    same_dest = decode_owner[:, :, None] == decode_owner[:, None, :]
    page_ranks = jnp.sum(jnp.logical_and(same_dest, earlier[None]), axis=-1)
    my_dest = decode_owner[my_group]
    my_rank = page_ranks[my_group]
    slot_ids = jnp.arange(groups * slot_cap)
    send_select = jnp.logical_and(
        my_dest[None, :] == (slot_ids // slot_cap)[:, None],
        my_rank[None, :] == (slot_ids % slot_cap)[:, None],
    ).astype(jnp.bfloat16)
    paged = new_kv.reshape(page_count, PAGE * kv_cols)
    outgoing = (
        jnp.dot(send_select, paged, preferred_element_type=jnp.float32)
        .astype(jnp.bfloat16)
        .reshape(groups, slot_cap * PAGE * kv_cols)
    )
    incoming = lax.all_to_all(outgoing, "group", split_axis=0, concat_axis=0, tiled=True)
    recv_select = jnp.logical_and(
        (decode_owner.T == my_group)[:, :, None],
        page_ranks.T[:, :, None] == jnp.arange(slot_cap)[None, None, :],
    )
    recv_select = recv_select.reshape(page_count, groups * slot_cap).astype(jnp.bfloat16)
    kv_pool = jnp.dot(
        recv_select,
        incoming.reshape(groups * slot_cap, PAGE * kv_cols),
        preferred_element_type=jnp.float32,
    )
    kv_pool = kv_pool.astype(jnp.bfloat16).reshape(page_count, PAGE, kv_cols)
    return (layer_out, kv_pool)


def solution(mesh):
    return jax.shard_map(
        local,
        mesh=mesh,
        in_specs=(
            P("group", None, "tensor", None),
            P(),
            P(None, "tensor"),
            P(None, "tensor"),
            P(None, "tensor"),
            P("tensor", None),
            P("group", None, "tensor"),
            P("group", None, None),
            P(),
            P(),
            P(),
        ),
        out_specs=(P(("group", "tensor"), None), P("group", None, "tensor")),
        check_vma=False,
    )
```

profile of v0, /device:TPU:0, one launch (start us, length us, event | category | flops | bytes accessed | tf_op | source)
XLA Modules:
  0.0 210.2 jit_solution(16953681199571292047)
XLA Ops:
  7.2 1.0 slice_bitcast_fusion.1
  9.2 11.6 %gather_fusion = bf16[1024,8,256]{2,1,0:T(8,128)(2,1)} fusion(bf16[2048,8,256]{2,1,0:T(8,128)(2,1)} %param.19, s32[1024]{0:T(1024)S(1)} %fusion.51), kind=kCustom, calls=%fused_computation.clone | custom fusion | bytes 8392704 | tf_op jit(solution)/shard_map/jit(_take)/gather | solution.py:107
  20.8 6.7 %select_bitcast_fusion = bf16[8192,256]{1,0:T(8,128)(2,1)} fusion(bf16[1024,8,256]{2,1,0:T(8,128)(2,1)} %gather_fusion, pred[1024]{0:T(1024)(128)(4,1)S(1)} %compare_and_fusion.2), kind=kLoop, calls=%fused_computation.15 | loop fusion | flops 2097152 | bytes 8389632 | tf_op jit(solution)/shard_map/reshape | solution.py:107
  31.3 11.6 %gather_fusion.1 = bf16[1024,8,256]{2,1,0:T(8,128)(2,1)} fusion(bf16[2048,8,256]{2,1,0:T(8,128)(2,1)} %param.19, s32[1024]{0:T(1024)S(1)} %fusion.52), kind=kCustom, calls=%fused_computation.1.clone | custom fusion | bytes 8392704 | tf_op jit(solution)/shard_map/jit(_take)/gather | solution.py:106
  44.1 1.2 multiply_cosine_fusion
  45.4 7.0 %fusion.7 = pred[256,8448]{0,1:T(8,128)(4,1)S(1)} fusion(s32[8448]{0:T(1024)S(1)} %iota_add_fusion, pred[8448]{0:T(1024)(128)(4,1)S(1)} %iota_compare_fusion.1, pred[8448]{0:T(1024)(128)(4,1)S(1)} %iota_compare_fusion.2), kind=kLoop, calls=%fused_computation.11 | loop fusion | flops 4325376 | bytes 2213376 | tf_op jit(solution)/shard_map/vmap(jit(_where))/select_n | solution.py:73
  52.4 21.3 %all-gather.3.cloned.1.call-done = bf16[256,4096]{1,0:T(8,128)(2,1)} async-done(((bf16[32,4096]{1,0:T(8,128)(2,1)}), bf16[256,4096]{1,0:T(8,128)(2,1)}) %all-gather.3.cloned.1.call-update) | async-done | bytes 2097168 | tf_op jit(solution)/shard_map/all_gather | solution.py:119
  73.7 2.5 %fusion.62 = f32[256,128]{1,0:T(8,128)S(1)} fusion(bf16[256,4096]{1,0:T(8,128)(2,1)} %all-gather.3.cloned.1.call-done, bf16[4096,128]{1,0:T(8,128)(2,1)S(1)} %copy-done), kind=kOutput, calls=%fused_computation.107 | convolution fusion | flops 268435456 | bytes 3276800 | tf_op jit(solution)/shard_map/dot_general | solution.py:124
  76.2 2.5 %fusion.63 = f32[256,128]{1,0:T(8,128)S(1)} fusion(bf16[256,4096]{1,0:T(8,128)(2,1)} %all-gather.3.cloned.1.call-done, bf16[4096,128]{1,0:T(8,128)(2,1)} %param.17), kind=kOutput, calls=%fused_computation.108 | convolution fusion | flops 268435456 | bytes 3276800 | tf_op jit(solution)/shard_map/dot_general | solution.py:125
  78.8 1.2 fusion.61
  80.1 0.9 copy-done.4
  81.0 0.8 slice.67
  81.9 1.2 reshape.471
  83.1 0.9 fusion.45
  84.8 1.1 slice_bitcast_fusion.2
  85.8 1.2 fusion.39
  87.4 1.1 fusion.29
  88.5 6.7 %bitcast_select_fusion.1 = bf16[8192,256]{1,0:T(8,128)(2,1)} fusion(bf16[8192,256]{1,0:T(8,128)(2,1)} %collective-permute-done.1, bf16[1024,8,256]{2,1,0:T(8,128)(2,1)S(1)} %copy-done.2, pred[1024]{0:T(1024)(128)(4,1)S(1)} %compare_and_fusion.1, pred[]{:T(512)S(6)} %eq.80), kind=kLoop, calls=%fused_computation.14 | loop fusion | flops 4194304 | bytes 12583937 | tf_op jit(solution)/shard_map/jit(_where)/select_n | solution.py:39
  95.2 6.4 %copy.60 = bf16[8192,256]{0,1:T(8,128)(2,1)} copy(bf16[8192,256]{1,0:T(8,128)(2,1)} %bitcast_select_fusion.1) | data formatting | bytes 8388608 | tf_op jit(solution)/shard_map/jit(_where)/select_n | solution.py:39
  101.6 4.6 %slice_bitcast_fusion = (bf16[1,8192,1,128]{1,3,2,0:T(8,128)(2,1)}, bf16[1,8192,1,1,128]{1,4,3,2,0:T(8,128)(2,1)}) fusion(bf16[1,8192,1,2,128]{1,4,3,2,0:T(8,128)(2,1)} %bitcast.121), kind=kLoop, calls=%fused_computation.27 | loop fusion | bytes 8388608 | tf_op jit(solution)/shard_map/vmap()/squeeze | solution.py:70
  106.3 4.2 %copy.73 = bf16[1,8192,1,1,128]{4,1,3,2,0:T(8,128)(2,1)} copy(bf16[1,8192,1,1,128]{1,4,3,2,0:T(8,128)(2,1)} %get-tuple-element.6) | data formatting | bytes 4194304
  110.4 15.5 %fusion.2 = (f32[4,256]{1,0:T(4,128)S(1)}, f32[8448,256,4]{1,0,2:T(8,128)}) fusion(pred[256,8448]{0,1:T(8,128)(4,1)S(1)} %fusion.7, bf16[256,4,64]{2,0,1:T(8,128)(2,1)S(1)} %get-tuple-element.8, bf16[256,4,64]{2,0,1:T(8,128)(2,1)S(1)} %get-tuple-element.7, bf16[1,256,1,64]{3,1,2,0:T(8,128)(2,1)S(1)} %copy-done.8, bf16[1,256,1,64]{3,1,2,0:T(8,128)(2,1)S(1)} %copy-done.6, ...), kind=kOutput, calls=%fused_computation.6 | convolution fusion | flops 2247556096 | bytes 39194624 | tf_op jit(solution)/shard_map/vmap(qhgd,khd->hgqk)/dot_general | solution.py:45
  125.9 14.8 %fusion = f32[4,256]{1,0:T(4,128)S(1)} fusion(f32[8448,256,4]{1,0,2:T(8,128)} %get-tuple-element.20, f32[4,256]{1,0:T(4,128)S(1)} %get-tuple-element.19, pred[256,8448]{0,1:T(8,128)(4,1)S(1)} %fusion.7), kind=kLoop, calls=%fused_computation.4 | loop fusion | flops 34601984 | bytes 36773888 | tf_op jit(solution)/shard_map/vmap()/reduce_sum | solution.py:51
  140.7 15.5 %fusion.22 = bf16[1,256,1,4,128]{1,4,3,2,0:T(8,128)(2,1)S(1)} fusion(f32[8448,256,4]{1,0,2:T(8,128)} %get-tuple-element.20, f32[4,256]{1,0:T(4,128)S(1)} %get-tuple-element.19, pred[256,8448]{0,1:T(8,128)(4,1)S(1)} %fusion.7, bf16[1,256,1,128]{1,3,2,0:T(8,128)(2,1)S(1)} %copy-done.11, bf16[1,8192,1,128]{1,3,2,0:T(8,128)(2,1)} %get-tuple-element.5, ...), kind=kOutput, calls=%fused_computation.30 | convolution fusion | flops 2253783040 | bytes 39198720 | tf_op jit(solution)/shard_map/vmap(hgqk,khd->qhgd)/dot_general | solution.py:52
  156.2 4.8 %fusion.8 = bf16[256,1,4096]{2,0,1:T(8,128)(2,1)} fusion(bf16[256,512]{0,1:T(8,128)(2,1)S(1)} %bitcast.124, bf16[512,4096]{1,0:T(8,128)(2,1)} %param.18), kind=kOutput, calls=%fused_computation.13 | convolution fusion | flops 1074790400 | bytes 6553600 | tf_op jit(solution)/shard_map/bsc,cd->bsd/dot_general | solution.py:153
  163.5 2.2 %reduce.5 = bf16[32,4096]{1,0:T(8,128)(2,1)S(1)} reduce(bf16[32,1,4096]{2,1,0:T(2,128)(2,1)S(1)} %all_to_all.8, bf16[]{:T(256)} %broadcast.313), dimensions={1}, to_apply=%all_to_all.8.reduce_sub_computation | reduce | bytes 524290 | tf_op jit(solution)/shard_map/all_to_all | solution.py:184
  165.7 0.9 reshape.504
  166.6 7.2 %all-to-all-start = ((bf16[32,2,2048]{2,1,0:T(2,128)(2,1)}), bf16[32,2,2048]{2,1,0:T(2,128)(2,1)S(1)}, u32[]{:S(2)}, u32[]{:S(2)}) async-start(bf16[32,2,2048]{2,1,0:T(2,128)(2,1)} %reshape.504), calls=%async_computation.1 | async-start | bytes 524288 | tf_op jit(solution)/shard_map/all_to_all | solution.py:184
  173.9 8.8 %all-to-all-done = bf16[32,2,2048]{2,1,0:T(2,128)(2,1)S(1)} async-done(((bf16[32,2,2048]{2,1,0:T(2,128)(2,1)}), bf16[32,2,2048]{2,1,0:T(2,128)(2,1)S(1)}, u32[]{:S(2)}, u32[]{:S(2)}) %all-to-all-start) | async-done | bytes 262176 | tf_op jit(solution)/shard_map/all_to_all | solution.py:184
  183.0 1.5 reduce.4
  185.5 16.2 %reduce-scatter.2.cloned.1.call-done = bf16[32,1,4096]{2,0,1:T(8,128)(2,1)} async-done(((bf16[256,1,4096]{2,0,1:T(8,128)(2,1)}), bf16[32,1,4096]{2,0,1:T(8,128)(2,1)}) %reduce-scatter.2.cloned.1.call-update) | async-done | bytes 262160 | tf_op jit(solution)/shard_map/reduce_scatter | solution.py:152
  201.7 1.7 fusion.28
  (77 shorter events, 8.9 us)
Async XLA Ops:
  7.2 66.6 %copy-start = (bf16[4096,128]{1,0:T(8,128)(2,1)S(1)}, bf16[4096,128]{1,0:T(8,128)(2,1)}, u32[]{:S(2)}) copy-start(bf16[4096,128]{1,0:T(8,128)(2,1)} %param.16) | copy-start | bytes 3145732
  7.2 66.6 %all-gather.3.cloned.1.call-start = ((), (), s32[]{:S(2)}) async-start(), calls=%async_computation.3 | async-start | bytes 2359296 | tf_op jit(solution)/shard_map/all_gather | solution.py:119
  8.3 20.5 %collective-permute-start = (bf16[32,4096]{1,0:T(8,128)(2,1)S(1)}, bf16[32,4096]{1,0:T(8,128)(2,1)S(1)}, u32[]{:S(2)}, u32[]{:S(2)}) collective-permute-start(bf16[32,4096]{1,0:T(8,128)(2,1)S(1)} %slice_bitcast_fusion.1), channel_id=1, source_target_pairs={{248,0},{0,8},{8,16},{16,24},{24,32},{32,40},{40,48},{48,56},{56,6... | collective-permute-start | bytes 786440 | tf_op jit(solution)/shard_map/ppermute | solution.py:21
  20.8 6.7 %copy-start.12 = (bf16[4096]{0:T(1024)(128)(2,1)S(1)}, bf16[4096]{0:T(1024)(128)(2,1)}, u32[]{:S(2)}) copy-start(bf16[4096]{0:T(1024)(128)(2,1)} %param.14) | copy-start | bytes 24580
  20.8 6.7 %copy-start.15 = (s32[32]{0:T(128)S(1)}, s32[32]{0:T(128)}, u32[]{:S(2)}) copy-start(s32[32]{0:T(128)} %param.22) | copy-start | bytes 388
  20.8 8.0 %copy-start.5 = (bf16[1,2,32,4096]{3,2,1,0:T(8,128)(2,1)S(1)}, bf16[1,2,32,4096]{3,2,1,0:T(8,128)(2,1)}, u32[]{:S(2)}) copy-start(bf16[1,2,32,4096]{3,2,1,0:T(8,128)(2,1)} %param.13) | copy-start | bytes 1572868
  20.8 9.3 %copy-start.13 = (s32[32,2]{0,1:T(2,128)S(1)}, s32[32,2]{0,1:T(2,128)}, u32[]{:S(2)}) copy-start(s32[32,2]{0,1:T(2,128)} %param.21) | copy-start | bytes 772
  27.5 61.1 %collective-permute-start.1 = (bf16[8192,256]{1,0:T(8,128)(2,1)}, bf16[8192,256]{1,0:T(8,128)(2,1)}, u32[]{:S(2)}, u32[]{:S(2)}) collective-permute-start(bf16[8192,256]{1,0:T(8,128)(2,1)} %select_bitcast_fusion), channel_id=1, source_target_pairs={{248,0},{0,8},{8,16},{16,24},{24,32},{32,40},{40,48},{48,56},{56,6... | collective-permute-start | bytes 12582920 | tf_op jit(solution)/shard_map/ppermute | solution.py:21
  29.8 171.8 %reduce-scatter.2.cloned.1.call-start = ((), (), s32[]{:S(2)}) async-start(), calls=%async_computation.2 | async-start | bytes 2359296 | tf_op jit(solution)/shard_map/reduce_scatter | solution.py:152
  73.7 5.0 %copy-start.3 = (bf16[256,4096]{1,0:T(8,128)(2,1)S(1)}, bf16[256,4096]{1,0:T(8,128)(2,1)}, u32[]{:S(2)}) copy-start(bf16[256,4096]{1,0:T(8,128)(2,1)} %all-gather.3.cloned.1.call-done) | copy-start | bytes 6291460
  73.7 5.0 %copy-start.14 = (bf16[4096,512]{1,0:T(8,128)(2,1)S(1)}, bf16[4096,512]{1,0:T(8,128)(2,1)}, u32[]{:S(2)}) copy-start(bf16[4096,512]{1,0:T(8,128)(2,1)} %param.15) | copy-start | bytes 12582916
  80.1 0.9 copy-start.4
  84.8 3.8 %copy-start.2 = (bf16[1024,8,256]{2,1,0:T(8,128)(2,1)S(1)}, bf16[1024,8,256]{2,1,0:T(8,128)(2,1)}, u32[]{:S(2)}) copy-start(bf16[1024,8,256]{2,1,0:T(8,128)(2,1)} %gather_fusion.1) | copy-start | bytes 12582916
  106.3 4.2 %copy-start.6 = (bf16[1,256,1,64]{3,1,2,0:T(8,128)(2,1)S(1)}, bf16[1,256,1,64]{3,1,2,0:T(8,128)(2,1)}, u32[]{:S(2)}) copy-start(bf16[1,256,1,64]{3,1,2,0:T(8,128)(2,1)} %get-tuple-element.13) | copy-start | bytes 98308
  106.3 4.2 %copy-start.8 = (bf16[1,256,1,64]{3,1,2,0:T(8,128)(2,1)S(1)}, bf16[1,256,1,64]{3,1,2,0:T(8,128)(2,1)}, u32[]{:S(2)}) copy-start(bf16[1,256,1,64]{3,1,2,0:T(8,128)(2,1)} %get-tuple-element.14) | copy-start | bytes 98308
  125.9 14.8 %copy-start.11 = (bf16[1,256,1,128]{1,3,2,0:T(8,128)(2,1)S(1)}, bf16[1,256,1,128]{1,3,2,0:T(8,128)(2,1)}, u32[]{:S(2)}) copy-start(bf16[1,256,1,128]{1,3,2,0:T(8,128)(2,1)} %copy.63) | copy-start | bytes 196612
  156.2 4.9 %copy-start.10 = (s32[32,32]{1,0:T(8,128)S(1)}, s32[32,32]{1,0:T(8,128)}, u32[]{:S(2)}) copy-start(s32[32,32]{1,0:T(8,128)} %param.23) | copy-start | bytes 12292
  156.2 5.7 %copy-start.7 = (bf16[1,256,1,64]{3,1,2,0:T(8,128)(2,1)S(1)}, bf16[1,256,1,64]{3,1,2,0:T(8,128)(2,1)}, u32[]{:S(2)}) copy-start(bf16[1,256,1,64]{3,1,2,0:T(8,128)(2,1)} %get-tuple-element.13) | copy-start | bytes 98308
  156.2 5.7 %copy-start.9 = (bf16[1,256,1,64]{3,1,2,0:T(8,128)(2,1)S(1)}, bf16[1,256,1,64]{3,1,2,0:T(8,128)(2,1)}, u32[]{:S(2)}) copy-start(bf16[1,256,1,64]{3,1,2,0:T(8,128)(2,1)} %get-tuple-element.14) | copy-start | bytes 98308
  161.1 42.3 %copy-start.1 = (bf16[4096,128]{1,0:T(8,128)(2,1)S(1)}, bf16[4096,128]{1,0:T(8,128)(2,1)}, u32[]{:S(2)}) copy-start(bf16[4096,128]{1,0:T(8,128)(2,1)} %param.16) | copy-start | bytes 3145732
  166.6 16.1 %all-to-all-start = ((bf16[32,2,2048]{2,1,0:T(2,128)(2,1)}), bf16[32,2,2048]{2,1,0:T(2,128)(2,1)S(1)}, u32[]{:S(2)}, u32[]{:S(2)}) async-start(bf16[32,2,2048]{2,1,0:T(2,128)(2,1)} %reshape.504), calls=%async_computation.1 | async-start | bytes 524288 | tf_op jit(solution)/shard_map/all_to_all | solution.py:184
Sparse Core Ops, SparseCore 0:
  30.0 43.7 all-gather.2
  161.2 40.4 reduce-scatter.1
where the time goes:
time: 213 us; the launch traced here: 210 us
  local copies, waits for them, and re-layouts  50.4 us (24%)
  other arithmetic  47.1 us (22%)
  waiting for transfers between devices  46.3 us (22%)
  matrix products  42.5 us (20%)
  between operations  16.3 us (8%)
  starting transfers between devices  7.52 us (4%)
    all_gather x1, waiting for transfers between devices, local(): piece = lax.all_gather(normed, 'tensor', axis=1, tiled=True)  21.3 us
    reduce_scatter x1, waiting for transfers between devices, local(): lax.psum_scatter(jnp.einsum('bsc,cd->bsd', by_rows, w_output, preferred_e...  16.2 us
    dot_general x1, matrix products, attend(): jnp.einsum('hgqk,khd->qhgd', exp_scores.astype(jnp.bfloat16), all_values,...  15.5 us
    dot_general x1, matrix products, attend(): jnp.einsum('qhgd,khd->hgqk', grouped, all_keys, preferred_element_type=jn...  15.5 us
    reduce_sum x1, other arithmetic, attend(): row_total = jnp.sum(exp_scores, axis=-1)  14.8 us
    gather x1, local copies, waits for them, and re-layouts, local(): jnp.take(prefix_pool, region + page_table[0, 1], axis=0)  11.6 us
    gather x1, local copies, waits for them, and re-layouts, local(): jnp.take(prefix_pool, page_table[0, 0], axis=0).reshape(PREFIX, kv_cols)  11.6 us
    all_to_all x1, waiting for transfers between devices, local(): lax.all_to_all(outgoing, 'group', split_axis=0, concat_axis=0, tiled=True)  8.81 us
  transfers between devices with their start and end apart: 5, of which 3 were waited for; matrix products, arithmetic and copies ran while one was open for 30% of the time, Pallas kernels for 0%

commit v1 on v0

v1 whole, which is shorter than its diff:
```python
import functools
import math

import jax
import jax.numpy as jnp
from jax import lax
from jax.experimental import pallas as pl
from jax.experimental.pallas import tpu as pltpu
from jax.sharding import PartitionSpec as P

HD = 128
PAGE = 8
BLOCK = 256
PREFIX = 8192
EPS = 1e-05
THETA = 500000.0

NT = 8
HEADS = 4
SHARD = BLOCK // NT
TILE = 256
KBLK = 1024
NKB = PREFIX // KBLK
KEYS = PREFIX + BLOCK
NCH = 4
CHROWS = PREFIX // NCH
MASKED = -1e30
EXP_SCALE = math.log2(math.e) / math.sqrt(HD)
MIB = 1 << 20
F32 = jnp.float32
BF16 = jnp.bfloat16

VMEM = pl.BlockSpec(memory_space=pltpu.VMEM)
SMEM = pl.BlockSpec(memory_space=pltpu.SMEM)
ANY = pl.BlockSpec(memory_space=pl.ANY)


def shift(value, axis, distance):
    count = lax.axis_size(axis)
    return lax.ppermute(value, axis, [(i, (i + distance) % count) for i in range(count)])


def norm_kernel(take_ref, own_ref, handed_ref, gain_ref, rows_ref, normed_ref):
    take = take_ref[0] != 0
    rows = jnp.where(take, handed_ref[...].astype(F32), own_ref[...].astype(F32))
    rows_ref[...] = rows.astype(BF16)
    mean_square = jnp.mean(rows * rows, axis=-1, keepdims=True)
    normed_ref[...] = (rows * lax.rsqrt(mean_square + EPS) * gain_ref[...].astype(F32)).astype(BF16)


def choose_and_norm(take, own, handed, gain):
    return pl.pallas_call(
        norm_kernel,
        out_shape=[jax.ShapeDtypeStruct(own.shape, BF16)] * 2,
        in_specs=[SMEM, VMEM, VMEM, VMEM],
        out_specs=[VMEM, VMEM],
        compiler_params=pltpu.CompilerParams(vmem_limit_bytes=8 * MIB),
        cost_estimate=pl.CostEstimate(flops=10**6, bytes_accessed=10**6, transcendentals=0),
        name="choose_and_norm",
    )(take, own, handed, gain)


def qkv_kernel(z_ref, *refs):
    shards = refs[:NT]
    cos_ref, sin_ref, wq_hbm, wk_hbm, wv_hbm, q_ref, kv_ref, x_ref, wq_ref, wk_ref, wv_ref, sems = refs[NT:]
    copies = [
        pltpu.make_async_copy(src, dst, sems.at[n])
        for n, (src, dst) in enumerate([(wk_hbm, wk_ref), (wv_hbm, wv_ref)])
    ]
    half = wq_hbm.shape[0] // 2
    copies += [
        pltpu.make_async_copy(wq_hbm.at[pl.ds(n * half, half)], wq_ref.at[pl.ds(n * half, half)], sems.at[2 + n])
        for n in range(2)
    ]
    for copy in copies:
        copy.start()
    z = z_ref[0]
    for relative, shard in enumerate(shards):
        place = lax.rem(z + relative, NT)
        x_ref[pl.ds(pl.multiple_of(place * SHARD, SHARD), SHARD), :] = shard[...]
    cosine = cos_ref[...]
    sine = sin_ref[...]

    def rotated(values):
        return values * cosine + pltpu.roll(values, HD // 2, 1) * sine

    copies[0].wait()
    kv_ref[:, :HD] = rotated(jnp.dot(x_ref[...], wk_ref[...], preferred_element_type=F32)).astype(BF16)
    copies[1].wait()
    kv_ref[:, HD:] = jnp.dot(x_ref[...], wv_ref[...], preferred_element_type=F32).astype(BF16)
    copies[2].wait()
    copies[3].wait()
    for pair in range(HEADS // 2):
        both = jnp.dot(x_ref[...], wq_ref[:, pair * 2 * HD : (pair + 1) * 2 * HD], preferred_element_type=F32)
        for one in range(2):
            head = rotated(both[:, one * HD : (one + 1) * HD]).astype(BF16)
            n = pair * 2 + one
            for shard in range(NT):
                q_ref[shard, n * SHARD : (n + 1) * SHARD, :] = head[shard * SHARD : (shard + 1) * SHARD, :]


def project(z, shards, cosine, sine, w_query, w_key, w_value):
    depth, query_width = w_query.shape
    return pl.pallas_call(
        qkv_kernel,
        out_shape=[
            jax.ShapeDtypeStruct((NT, HEADS * SHARD, HD), BF16),
            jax.ShapeDtypeStruct((BLOCK, 2 * HD), BF16),
        ],
        in_specs=[SMEM] + [VMEM] * (NT + 2) + [ANY] * 3,
        out_specs=[VMEM, VMEM],
        scratch_shapes=[
            pltpu.VMEM((BLOCK, depth), BF16),
            pltpu.VMEM(w_query.shape, BF16),
            pltpu.VMEM(w_key.shape, BF16),
            pltpu.VMEM(w_value.shape, BF16),
            pltpu.SemaphoreType.DMA((4,)),
        ],
        compiler_params=pltpu.CompilerParams(vmem_limit_bytes=28 * MIB),
        cost_estimate=pl.CostEstimate(
            flops=2 * BLOCK * depth * (query_width + 2 * HD), bytes_accessed=9 * 10**6, transcendentals=0
        ),
        name="project",
    )(z, *shards, cosine, sine, w_query, w_key, w_value)


def attention_kernel(tiles, picks, info_ref, q_ref, new_ref, bias_ref, wo_hbm, pool_hbm, *refs):
    handed = refs[:NCH]
    out_ref, kv_ref, s_ref, att_ref, wo_ref, kv_sem, wo_sem = refs[NCH:]
    z = info_ref[0]
    take = info_ref[1]

    def cache_copy(n, source):
        return pltpu.make_async_copy(source, kv_ref.at[pl.ds(n * CHROWS, CHROWS)], kv_sem.at[n])

    @pl.when(take != 0)
    def _():
        for n in range(NCH):
            cache_copy(n, handed[n]).start()

    @pl.when(take == 0)
    def _():
        for n in range(NCH):
            cache_copy(n, pool_hbm.at[pl.ds(n * CHROWS, CHROWS)]).start()

    wo_copy = pltpu.make_async_copy(wo_hbm, wo_ref, wo_sem)
    wo_copy.start()

    def shard_of(tile, half):
        return lax.rem(z + picks[2 * tile + half], NT)

    def query_tile(tile):
        return jnp.concatenate([q_ref[shard_of(tile, 0)], q_ref[shard_of(tile, 1)]], axis=0)

    def scores(queries, keys):
        return lax.dot_general(queries, keys, (((1,), (1,)), ((), ())), preferred_element_type=F32)

    def fold_max(block, running):
        for n in range(block.shape[1] // HD):
            running = jnp.maximum(running, block[:, n * HD : (n + 1) * HD])
        return running

    def score_block(tile, queries, n, running):
        at = pl.multiple_of(n * KBLK, KBLK)
        block = scores(queries, kv_ref[pl.ds(at, KBLK), :HD]) + bias_ref[:, pl.ds(at, KBLK)]
        s_ref[tile % 2, :, pl.ds(at, KBLK)] = block
        return fold_max(block, running)

    def score_new(tile, queries, running):
        block = scores(queries, new_ref[:, :HD])
        place = lax.broadcasted_iota(jnp.int32, (TILE, BLOCK), 0)
        row = place % SHARD + SHARD * jnp.where(place < TILE // 2, shard_of(tile, 0), shard_of(tile, 1))
        column = lax.broadcasted_iota(jnp.int32, (TILE, BLOCK), 1)
        block = jnp.where(column <= row, block, MASKED)
        s_ref[tile % 2, :, PREFIX:] = block
        return fold_max(block, running)

    def weigh(tile, at, width, row_max, values, total, sums):
        e = jnp.exp2((s_ref[tile % 2, :, pl.ds(at, width)] - row_max) * EXP_SCALE)
        for n in range(width // HD):
            total = total + e[:, n * HD : (n + 1) * HD]
        return total, sums + jnp.dot(e.astype(BF16), values, preferred_element_type=F32)

    lowest = jnp.full((TILE, HD), MASKED, F32)
    zeros = jnp.zeros((TILE, HD), F32)
    per = KBLK and CHROWS // KBLK
    running = lowest
    queries = query_tile(0)
    for n in range(NKB):
        if n % per == 0:
            cache_copy(n // per, pool_hbm.at[pl.ds((n // per) * CHROWS, CHROWS)]).wait()
        running = score_block(0, queries, n, running)
    running = score_new(0, queries, running)
    for tile in range(tiles):
        row_max = jnp.max(running, axis=1, keepdims=True)
        last = tile == tiles - 1
        queries = None if last else query_tile(tile + 1)

        def step(n, carry):
            running, total, sums = carry
            at = pl.multiple_of(n * KBLK, KBLK)
            if not last:
                running = score_block(tile + 1, queries, n, running)
            total, sums = weigh(tile, at, KBLK, row_max, kv_ref[pl.ds(at, KBLK), HD:], total, sums)
            return running, total, sums

        running, total, sums = lax.fori_loop(0, NKB, step, (lowest, zeros, zeros))
        if not last:
            running = score_new(tile + 1, queries, running)
        total, sums = weigh(tile, PREFIX, BLOCK, row_max, new_ref[:, HD:], total, sums)
        attended = (sums / jnp.sum(total, axis=1, keepdims=True)).astype(BF16)
        for half in range(2):
            for n in range(HEADS):
                at = half * HEADS * SHARD + n * SHARD
                to = (2 * tile + half) * SHARD
                att_ref[to : to + SHARD, n * HD : (n + 1) * HD] = attended[at : at + SHARD, :]
    wo_copy.wait()
    out_ref[...] = jnp.dot(att_ref[...], wo_ref[...], preferred_element_type=F32).astype(BF16)


def attend(info, picks, queries, new_kv, bias, w_output, pool, handed):
    tiles = len(picks) // 2
    rows = len(picks) * SHARD
    width = w_output.shape[1]
    return pl.pallas_call(
        functools.partial(attention_kernel, tiles, picks),
        out_shape=jax.ShapeDtypeStruct((rows, width), BF16),
        in_specs=[SMEM, VMEM, VMEM, VMEM, ANY, ANY] + [ANY] * NCH,
        out_specs=VMEM,
        scratch_shapes=[
            pltpu.VMEM((PREFIX, 2 * HD), BF16),
            pltpu.VMEM((2, TILE, KEYS), F32),
            pltpu.VMEM((rows, HEADS * HD), BF16),
            pltpu.VMEM(w_output.shape, BF16),
            pltpu.SemaphoreType.DMA((NCH,)),
            pltpu.SemaphoreType.DMA,
        ],
        compiler_params=pltpu.CompilerParams(vmem_limit_bytes=48 * MIB),
        cost_estimate=pl.CostEstimate(
            flops=4 * tiles * TILE * KEYS * HD, bytes_accessed=9 * 10**6, transcendentals=tiles * TILE * KEYS
        ),
        name="attend",
    )(info, queries, new_kv, bias, w_output, pool, *handed)


def pick_kernel(source_ref, pages_hbm, out_hbm, sem):
    count = out_hbm.shape[0]

    def copy(k, source):
        return pltpu.make_async_copy(pages_hbm.at[source], out_hbm.at[k], sem)

    for k in range(count):
        copy(k, source_ref[k]).start()
    pltpu.make_async_copy(pages_hbm.at[pl.ds(0, count)], out_hbm, sem).wait()


def pick_pages(sources, pages, count):
    return pl.pallas_call(
        pick_kernel,
        out_shape=jax.ShapeDtypeStruct((count,) + pages.shape[1:], BF16),
        in_specs=[SMEM, ANY],
        out_specs=ANY,
        scratch_shapes=[pltpu.SemaphoreType.DMA],
        cost_estimate=pl.CostEstimate(flops=0, bytes_accessed=3 * 10**5, transcendentals=0),
        name="pick_pages",
    )(sources, pages)


def local(
    hidden,
    norm_gain,
    w_query,
    w_key,
    w_value,
    w_output,
    prefix_pool,
    page_table,
    prefix_len,
    source,
    decode_owner,
):
    groups = lax.axis_size("group")
    group = lax.axis_index("group")
    z = lax.axis_index("tensor")
    lower = (group + groups - 1) % groups
    take = source[group] == lower
    take_flag = take.astype(jnp.int32)
    count = jnp.where(take, prefix_len[lower, 1], prefix_len[group, 0])

    handed_rows = shift(hidden[0, 1], "group", 1)
    pages = prefix_pool.shape[0] // 2
    part = pages // NCH
    handed = [
        shift(prefix_pool[pages + n * part : pages + (n + 1) * part], "group", 1).reshape(CHROWS, 2 * HD)
        for n in range(NCH)
    ]
    handed_table = shift(page_table[0, 1], "group", 1)

    table = jnp.where(take, handed_table, page_table[0, 0])
    order = jnp.arange(pages, dtype=jnp.int32)
    place = jnp.sum(jnp.where(table[:, None] == order[None, :], order[:, None], 0), axis=0)
    position = place[:, None] * PAGE + jnp.arange(PAGE, dtype=jnp.int32)[None, :]
    bias = jnp.where(position < count, 0.0, MASKED).astype(F32).reshape(1, PREFIX)

    positions = (count + jnp.arange(BLOCK, dtype=jnp.int32)).astype(F32)
    frequency = THETA ** (-(jnp.arange(HD // 2, dtype=F32) * 2.0) / HD)
    angles = positions[:, None] * frequency
    cosine = jnp.cos(angles)
    sine = jnp.sin(angles)
    cosine = jnp.concatenate([cosine, cosine], axis=1)
    sine = jnp.concatenate([-sine, sine], axis=1)

    rows, normed = choose_and_norm(take_flag[None], hidden[0, 0], handed_rows, norm_gain[None])

    up, down = [normed], [normed]
    for _ in range(NT // 2 - 1):
        up.append(shift(up[-1], "tensor", 1))
        down.append(shift(down[-1], "tensor", -1))
    half = SHARD // 2
    opposite = jnp.concatenate([shift(up[-1][:half], "tensor", 1), shift(down[-1][half:], "tensor", -1)], axis=0)
    shards = down + [opposite] + up[:0:-1]
    queries, new_kv = project(z[None], shards, cosine, sine, w_query, w_key, w_value)

    page_count = BLOCK // PAGE
    everywhere = lax.all_gather(new_kv.reshape(page_count, PAGE, 2 * HD), "group", axis=0, tiled=True)
    sender = jnp.argmax(decode_owner == group, axis=0).astype(jnp.int32)
    kv_pool = pick_pages(sender * page_count + jnp.arange(page_count, dtype=jnp.int32), everywhere, page_count)

    info = jnp.stack([z.astype(jnp.int32), take_flag])
    pool = prefix_pool.reshape(2 * PREFIX, 2 * HD)
    first = attend(info, (4, 3, 5, 2), queries, new_kv, bias, w_output, pool, handed)
    second = attend(info, (6, 1, 7, 0), queries, new_kv, bias, w_output, pool, handed)
    parts = {}
    for n, pick in enumerate((4, 3, 5, 2)):
        parts[pick] = first[n * SHARD : (n + 1) * SHARD]
    for n, pick in enumerate((6, 1, 7, 0)):
        parts[pick] = second[n * SHARD : (n + 1) * SHARD]

    columns = w_output.shape[1] // 2
    going_up = shift(parts[4][:, :columns], "tensor", 1)
    going_down = shift(parts[4][:, columns:], "tensor", -1)

    def plus(a, b):
        return a.astype(F32) + b.astype(F32)

    next_up = jnp.concatenate(
        [plus(parts[3][:, :columns], going_up).astype(BF16), parts[3][:, columns:]], axis=1
    )
    next_down = jnp.concatenate(
        [parts[5][:, :columns], plus(parts[5][:, columns:], going_down).astype(BF16)], axis=1
    )
    for step in (2, 1):
        next_up = plus(parts[step], shift(next_up, "tensor", 1)).astype(BF16)
        next_down = plus(parts[NT - step], shift(next_down, "tensor", -1)).astype(BF16)
    branch = parts[0].astype(F32) + plus(shift(next_up, "tensor", 1), shift(next_down, "tensor", -1))
    layer_out = (rows.astype(F32) + branch).astype(BF16)
    return (layer_out, kv_pool)


def solution(mesh):
    return jax.shard_map(
        local,
        mesh=mesh,
        in_specs=(
            P("group", None, "tensor", None),
            P(),
            P(None, "tensor"),
            P(None, "tensor"),
            P(None, "tensor"),
            P("tensor", None),
            P("group", None, "tensor"),
            P("group", None, None),
            P(),
            P(),
            P(),
        ),
        out_specs=(P(("group", "tensor"), None), P("group", None, "tensor")),
        check_vma=False,
    )
```

time: 213 us -> 197 us (0.925)
  waiting for transfers between devices: 46.3 us -> 92.9 us
  matrix products: 42.5 us -> 0 us
  other arithmetic: 47.1 us -> 7.27 us
  Pallas kernels: 0 us -> 33.4 us
  local copies, waits for them, and re-layouts: 50.4 us -> 17 us
  starting transfers between devices: 7.52 us -> 29.4 us
    ppermute x2 -> x22, waiting for transfers between devices: 0.01 us -> 92.8 us  [shift(): lax.ppermute(value, axis, [(i, (i + distance) % count) for i in range(cou...]
    dot_general x8 -> x0, matrix products: 42.5 us -> none  [the longest x1 15.5 us: attend(): jnp.einsum('hgqk,khd->qhgd', exp_scores.astype(jnp.bfloat16), all_values,...]
    pallas_call x0 -> x5, Pallas kernels: none -> 33.4 us  [the longest x2 22.4 us: attend(): pl.pallas_call(functools.partial(attention_kernel, tiles, picks), out_sha...]
    ppermute x2 -> x22, starting transfers between devices: 0.09 us -> 29.4 us  [shift(): lax.ppermute(value, axis, [(i, (i + distance) % count) for i in range(cou...]
    gather x2 -> x0, local copies, waits for them, and re-layouts: 23.2 us -> none  [the longest x1 11.6 us: local(): jnp.take(prefix_pool, region + page_table[0, 1], axis=0)]
    all_gather x1, waiting for transfers between devices: 21.3 us -> 0.01 us  [local(): lax.all_gather(new_kv.reshape(page_count, PAGE, 2 * HD), 'group', axis=0,...]
    reduce_scatter x1 -> x0, waiting for transfers between devices: 16.2 us -> none  [local(): lax.psum_scatter(jnp.einsum('bsc,cd->bsd', by_rows, w_output, preferred_e...]
    reduce_sum x3 -> x1, other arithmetic: 15.8 us -> 0.5 us  [local(): jnp.sum(jnp.where(table[:, None] == order[None, :], order[:, None], 0), a...]
  transfers between devices with their start and end apart: 5 -> 23, of which waited for: 3 -> 12; matrix products, arithmetic and copies ran while one was open for 30% -> 8% of each run, Pallas kernels for 0% -> 11%
where the time goes in v1:
time: 197 us; the launch traced here: 196 us
  waiting for transfers between devices  92.9 us (47%)
  Pallas kernels  33.4 us (17%)
  starting transfers between devices  29.4 us (15%)
  local copies, waits for them, and re-layouts  17 us (9%)
  between operations  16.3 us (8%)
  other arithmetic  7.27 us (4%)
    ppermute x22, waiting for transfers between devices, shift(): lax.ppermute(value, axis, [(i, (i + distance) % count) for i in range(cou...  92.8 us
    ppermute x22, starting transfers between devices, shift(): lax.ppermute(value, axis, [(i, (i + distance) % count) for i in range(cou...  29.4 us
    pallas_call x2, Pallas kernels, attend(): pl.pallas_call(functools.partial(attention_kernel, tiles, picks), out_sha...  22.4 us
    pallas_call x1, Pallas kernels, pick_pages(): pl.pallas_call(pick_kernel, out_shape=jax.ShapeDtypeStruct((count,) + pag...  5.75 us
    unnamed x22, local copies, waits for them, and re-layouts  5.53 us
    pallas_call x1, Pallas kernels, project(): pl.pallas_call(qkv_kernel, out_shape=[jax.ShapeDtypeStruct((NT, HEADS * S...  5.01 us
    slice x1, local copies, waits for them, and re-layouts, local(): prefix_pool[pages + n * part:pages + (n + 1) * part]  4.29 us
  transfers between devices with their start and end apart: 23, of which 12 were waited for; matrix products, arithmetic and copies ran while one was open for 8% of the time, Pallas kernels for 11%

profile of v1, /device:TPU:0, one launch (start us, length us, event | category | flops | bytes accessed | tf_op | source)
XLA Modules:
  0.0 196.3 jit_solution(262768278811671072)
XLA Ops:
  7.2 1.2 slice_bitcast_fusion
  8.5 1.2 dynamic_slice.9
  11.1 6.5 %collective-permute-done.handed_ref = bf16[32,4096]{1,0:T(8,128)(2,1)S(1)} collective-permute-done((bf16[32,4096]{1,0:T(8,128)(2,1)S(1)}, bf16[32,4096]{1,0:T(8,128)(2,1)S(1)}, u32[]{:S(2)}, u32[]{:S(2)}) %collective-permute-start) | collective-permute-done | bytes 262176 | tf_op jit(solution)/shard_map/ppermute | solution.py:40
  18.6 4.1 %collective-permute-start.1 = (bf16[32,4096]{1,0:T(8,128)(2,1)S(1)}, bf16[32,4096]{1,0:T(8,128)(2,1)S(1)}, u32[]{:S(2)}, u32[]{:S(2)}) collective-permute-start(bf16[32,4096]{1,0:T(8,128)(2,1)S(1)} %get-tuple-element.8.refs_0_), channel_id=1, source_target_pairs={{0,7},{1,0},{2,1},{3,2},{4,3},{5,4},{6,5},{7,6},{8,15},{9,8},{10,9... | collective-permute-start | bytes 786440 | tf_op jit(solution)/shard_map/ppermute | solution.py:40
  22.7 5.4 %collective-permute-done.1.refs_1_ = bf16[32,4096]{1,0:T(8,128)(2,1)S(1)} collective-permute-done((bf16[32,4096]{1,0:T(8,128)(2,1)S(1)}, bf16[32,4096]{1,0:T(8,128)(2,1)S(1)}, u32[]{:S(2)}, u32[]{:S(2)}) %collective-permute-start.1) | collective-permute-done | bytes 262176 | tf_op jit(solution)/shard_map/ppermute | solution.py:40
  28.1 3.7 %collective-permute-start.2 = (bf16[32,4096]{1,0:T(8,128)(2,1)S(1)}, bf16[32,4096]{1,0:T(8,128)(2,1)S(1)}, u32[]{:S(2)}, u32[]{:S(2)}) collective-permute-start(bf16[32,4096]{1,0:T(8,128)(2,1)S(1)} %collective-permute-done.1.refs_1_), channel_id=1, source_target_pairs={{0,7},{1,0},{2,1},{3,2},{4,3},{5,4},{6,5},{7,6},{8,15},{9,8},{10,9... | collective-permute-start | bytes 786440 | tf_op jit(solution)/shard_map/ppermute | solution.py:40
  32.8 5.5 %collective-permute-done.2.refs_2_ = bf16[32,4096]{1,0:T(8,128)(2,1)S(1)} collective-permute-done((bf16[32,4096]{1,0:T(8,128)(2,1)S(1)}, bf16[32,4096]{1,0:T(8,128)(2,1)S(1)}, u32[]{:S(2)}, u32[]{:S(2)}) %collective-permute-start.2) | collective-permute-done | bytes 262176 | tf_op jit(solution)/shard_map/ppermute | solution.py:40
  38.3 3.7 %collective-permute-start.3 = (bf16[32,4096]{1,0:T(8,128)(2,1)S(1)}, bf16[32,4096]{1,0:T(8,128)(2,1)S(1)}, u32[]{:S(2)}, u32[]{:S(2)}) collective-permute-start(bf16[32,4096]{1,0:T(8,128)(2,1)S(1)} %collective-permute-done.2.refs_2_), channel_id=1, source_target_pairs={{0,7},{1,0},{2,1},{3,2},{4,3},{5,4},{6,5},{7,6},{8,15},{9,8},{10,9... | collective-permute-start | bytes 786440 | tf_op jit(solution)/shard_map/ppermute | solution.py:40
  42.4 1.3 constant_dynamic-slice_fusion.1
  45.0 2.3 %collective-permute-done.3.refs_3_ = bf16[32,4096]{1,0:T(8,128)(2,1)S(1)} collective-permute-done((bf16[32,4096]{1,0:T(8,128)(2,1)S(1)}, bf16[32,4096]{1,0:T(8,128)(2,1)S(1)}, u32[]{:S(2)}, u32[]{:S(2)}) %collective-permute-start.3) | collective-permute-done | bytes 262176 | tf_op jit(solution)/shard_map/ppermute | solution.py:40
  48.0 3.7 %collective-permute-start.8 = (bf16[16,4096]{1,0:T(8,128)(2,1)}, bf16[16,4096]{1,0:T(8,128)(2,1)}, u32[]{:S(2)}, u32[]{:S(2)}) collective-permute-start(bf16[16,4096]{1,0:T(8,128)(2,1)} %slice.94), channel_id=1, source_target_pairs={{0,7},{1,0},{2,1},{3,2},{4,3},{5,4},{6,5},{7,6},{8,15},{9,8},{10,9... | collective-permute-start | bytes 393224 | tf_op jit(solution)/shard_map/ppermute | solution.py:40
  52.3 1.2 fusion.1
  53.6 1.2 pad_maximum_fusion.3
  54.8 4.1 %collective-permute-done.7 = bf16[16,4096]{1,0:T(8,128)(2,1)} collective-permute-done((bf16[16,4096]{1,0:T(8,128)(2,1)}, bf16[16,4096]{1,0:T(8,128)(2,1)}, u32[]{:S(2)}, u32[]{:S(2)}) %collective-permute-start.7) | collective-permute-done | bytes 131104 | tf_op jit(solution)/shard_map/ppermute | solution.py:40
  58.8 1.0 pad_maximum_fusion.refs_4_
  59.9 2.2 %copy-done = bf16[4096,512]{1,0:T(8,128)(2,1)S(1)} copy-done((bf16[4096,512]{1,0:T(8,128)(2,1)S(1)}, bf16[4096,512]{1,0:T(8,128)(2,1)}, u32[]{:S(2)}) %copy-start) | copy-done | bytes 4194328
  63.9 5.0 %project.1 = (bf16[8,128,128]{2,1,0:T(8,128)(2,1)S(1)}, bf16[256,256]{1,0:T(8,128)(2,1)}) custom-call(s32[1]{0:T(128)} %bitcast.4.z_ref, bf16[32,4096]{1,0:T(8,128)(2,1)S(1)} %get-tuple-element.8.refs_0_, bf16[32,4096]{1,0:T(8,128)(2,1)S(1)} %collective-permute-done.1.refs_1_, bf16[32,4096]{1,0:T(8,128)(2,1)S(1)} %copy-done.8, ...), custom_call_target="tpu_custom_call" | custom-call | flops 1610612736 | bytes 9000000 | tf_op jit(solution)/shard_map/project/pallas_call | solution.py:104
  69.0 4.3 %fusion.2 = (bf16[256,8,256]{2,1,0:T(8,128)(2,1)}, bf16[256,8,256]{2,1,0:T(8,128)(2,1)}, bf16[256,8,256]{2,1,0:T(8,128)(2,1)}, bf16[256,8,256]{2,1,0:T(8,128)(2,1)}) fusion(bf16[2048,8,256]{2,1,0:T(8,128)(2,1)} %param.17), kind=kLoop, calls=%fused_computation.30 | loop fusion | bytes 8388608 | tf_op jit(solution)/shard_map/slice | solution.py:294
  73.7 53.2 %collective-permute-done.9 = s32[1024]{0:T(1024)S(1)} collective-permute-done((s32[1024]{0:T(1024)S(1)}, s32[1024]{0:T(1024)S(1)}, u32[]{:S(2)}, u32[]{:S(2)}) %collective-permute-start.9) | collective-permute-done | bytes 4128 | tf_op jit(solution)/shard_map/ppermute | solution.py:40
  127.4 1.0 fusion
  128.4 1.3 select_n.55.bias_ref
  129.7 11.1 %attend.3 = bf16[128,4096]{1,0:T(8,128)(2,1)S(1)} custom-call(s32[2]{0:T(128)S(1)} %pad_add_fusion.info_ref, bf16[8,128,128]{2,1,0:T(8,128)(2,1)S(1)} %get-tuple-element.9.q_ref, bf16[256,256]{1,0:T(8,128)(2,1)} %get-tuple-element.10.new_ref, f32[1,8192]{1,0:T(1,128)S(1)} %select_n.55.bias_ref, bf16[512,4096]{1,0:T(8,128)(2,1)} %wo_hbm.3, ...), custom_call_target="tpu_custom_call" | custom-call | flops 2214592512 | bytes 9000000 | tf_op jit(solution)/shard_map/attend/pallas_call | solution.py:225
  141.0 3.2 %collective-permute-start.18 = (bf16[32,2048]{1,0:T(8,128)(2,1)S(1)}, bf16[32,2048]{1,0:T(8,128)(2,1)S(1)}, u32[]{:S(2)}, u32[]{:S(2)}) collective-permute-start(bf16[32,2048]{1,0:T(8,128)(2,1)S(1)} %get-tuple-element.21), channel_id=1, source_target_pairs={{0,7},{1,0},{2,1},{3,2},{4,3},{5,4},{6,5},{7,6},{8,15},{9,8},{10,9... | collective-permute-start | bytes 393224 | tf_op jit(solution)/shard_map/ppermute | solution.py:40
  144.2 4.3 %collective-permute-done.14 = bf16[32,2048]{1,0:T(8,128)(2,1)S(1)} collective-permute-done((bf16[32,2048]{1,0:T(8,128)(2,1)S(1)}, bf16[32,2048]{1,0:T(8,128)(2,1)S(1)}, u32[]{:S(2)}, u32[]{:S(2)}) %collective-permute-start.14) | collective-permute-done | bytes 131104 | tf_op jit(solution)/shard_map/ppermute | solution.py:40
  148.7 3.3 %collective-permute-start.19 = (bf16[32,4096]{1,0:T(8,128)(2,1)S(1)}, bf16[32,4096]{1,0:T(8,128)(2,1)S(1)}, u32[]{:S(2)}, u32[]{:S(2)}) collective-permute-start(bf16[32,4096]{1,0:T(8,128)(2,1)S(1)} %pad_maximum_fusion.2), channel_id=1, source_target_pairs={{0,7},{1,0},{2,1},{3,2},{4,3},{5,4},{6,5},{7,6},{8,15},{9,8},{10,9... | collective-permute-start | bytes 786440 | tf_op jit(solution)/shard_map/ppermute | solution.py:40
  152.0 4.2 %collective-permute-done.15 = bf16[32,4096]{1,0:T(8,128)(2,1)S(1)} collective-permute-done((bf16[32,4096]{1,0:T(8,128)(2,1)S(1)}, bf16[32,4096]{1,0:T(8,128)(2,1)S(1)}, u32[]{:S(2)}, u32[]{:S(2)}) %collective-permute-start.15) | collective-permute-done | bytes 262176 | tf_op jit(solution)/shard_map/ppermute | solution.py:40
  156.4 11.3 %attend.2 = bf16[128,4096]{1,0:T(8,128)(2,1)S(1)} custom-call(s32[2]{0:T(128)S(1)} %pad_add_fusion.info_ref, bf16[8,128,128]{2,1,0:T(8,128)(2,1)S(1)} %get-tuple-element.9.q_ref, bf16[256,256]{1,0:T(8,128)(2,1)} %get-tuple-element.10.new_ref, f32[1,8192]{1,0:T(1,128)S(1)} %select_n.55.bias_ref, bf16[512,4096]{1,0:T(8,128)(2,1)} %wo_hbm.3, ...), custom_call_target="tpu_custom_call" | custom-call | flops 2214592512 | bytes 9000000 | tf_op jit(solution)/shard_map/attend/pallas_call | solution.py:225
  167.9 3.3 %collective-permute-start.20 = (bf16[32,4096]{1,0:T(8,128)(2,1)S(1)}, bf16[32,4096]{1,0:T(8,128)(2,1)S(1)}, u32[]{:S(2)}, u32[]{:S(2)}) collective-permute-start(bf16[32,4096]{1,0:T(8,128)(2,1)S(1)} %get-tuple-element.17), channel_id=1, source_target_pairs={{0,7},{1,0},{2,1},{3,2},{4,3},{5,4},{6,5},{7,6},{8,15},{9,8},{10,9... | collective-permute-start | bytes 786440 | tf_op jit(solution)/shard_map/ppermute | solution.py:40
  171.2 3.9 %collective-permute-done.20 = bf16[32,4096]{1,0:T(8,128)(2,1)S(1)} collective-permute-done((bf16[32,4096]{1,0:T(8,128)(2,1)S(1)}, bf16[32,4096]{1,0:T(8,128)(2,1)S(1)}, u32[]{:S(2)}, u32[]{:S(2)}) %collective-permute-start.20) | collective-permute-done | bytes 262176 | tf_op jit(solution)/shard_map/ppermute | solution.py:40
  175.1 3.8 %collective-permute-start.21 = (bf16[32,4096]{1,0:T(8,128)(2,1)S(1)}, bf16[32,4096]{1,0:T(8,128)(2,1)S(1)}, u32[]{:S(2)}, u32[]{:S(2)}) collective-permute-start(bf16[32,4096]{1,0:T(8,128)(2,1)S(1)} %add_convert_fusion.1), channel_id=1, source_target_pairs={{0,7},{1,0},{2,1},{3,2},{4,3},{5,4},{6,5},{7,6},{8,15},{9,8},{10,9... | collective-permute-start | bytes 786440 | tf_op jit(solution)/shard_map/ppermute | solution.py:40
  180.0 2.8 %collective-permute-done.21 = bf16[32,4096]{1,0:T(8,128)(2,1)S(1)} collective-permute-done((bf16[32,4096]{1,0:T(8,128)(2,1)S(1)}, bf16[32,4096]{1,0:T(8,128)(2,1)S(1)}, u32[]{:S(2)}, u32[]{:S(2)}) %collective-permute-start.21) | collective-permute-done | bytes 262176 | tf_op jit(solution)/shard_map/ppermute | solution.py:40
  183.6 5.7 %pick_pages.1 = bf16[32,8,256]{2,1,0:T(8,128)(2,1)} custom-call(s32[32]{0:T(128)} %iota_add_fusion.source_ref, bf16[1024,8,256]{2,1,0:T(8,128)(2,1)} %all-gather.2.cloned.1.call-done.pages_hbm), custom_call_target="tpu_custom_call" | custom-call | bytes 300000 | tf_op jit(solution)/shard_map/pick_pages/pallas_call | solution.py:258
  (71 shorter events, 10.0 us)
Async XLA Ops:
  7.2 52.7 %copy-start.1 = (bf16[4096,128]{1,0:T(8,128)(2,1)S(1)}, bf16[4096,128]{1,0:T(8,128)(2,1)}, u32[]{:S(2)}) copy-start(bf16[4096,128]{1,0:T(8,128)(2,1)} %refs_11_.1) | copy-start | bytes 3145732
  7.2 52.7 %copy-start.2 = (bf16[4096,128]{1,0:T(8,128)(2,1)S(1)}, bf16[4096,128]{1,0:T(8,128)(2,1)}, u32[]{:S(2)}) copy-start(bf16[4096,128]{1,0:T(8,128)(2,1)} %refs_12_.1) | copy-start | bytes 3145732
  7.2 176.5 %all-gather.2.cloned.1.call-start = ((), (), s32[]{:S(2)}) async-start(), calls=%async_computation | async-start | bytes 4325376 | tf_op jit(solution)/shard_map/all_gather | solution.py:325
  8.4 9.2 %collective-permute-start = (bf16[32,4096]{1,0:T(8,128)(2,1)S(1)}, bf16[32,4096]{1,0:T(8,128)(2,1)S(1)}, u32[]{:S(2)}, u32[]{:S(2)}) collective-permute-start(bf16[32,4096]{1,0:T(8,128)(2,1)S(1)} %get-tuple-element.24), channel_id=1, source_target_pairs={{0,8},{8,16},{16,24},{24,32},{32,40},{40,48},{48,56},{56,64},{64,7... | collective-permute-start | bytes 786440 | tf_op jit(solution)/shard_map/ppermute | solution.py:40
  18.6 9.5 %collective-permute-start.1 = (bf16[32,4096]{1,0:T(8,128)(2,1)S(1)}, bf16[32,4096]{1,0:T(8,128)(2,1)S(1)}, u32[]{:S(2)}, u32[]{:S(2)}) collective-permute-start(bf16[32,4096]{1,0:T(8,128)(2,1)S(1)} %get-tuple-element.8.refs_0_), channel_id=1, source_target_pairs={{0,7},{1,0},{2,1},{3,2},{4,3},{5,4},{6,5},{7,6},{8,15},{9,8},{10,9... | collective-permute-start | bytes 786440 | tf_op jit(solution)/shard_map/ppermute | solution.py:40
  22.7 9.4 %collective-permute-start.4 = (bf16[32,4096]{1,0:T(8,128)(2,1)S(1)}, bf16[32,4096]{1,0:T(8,128)(2,1)S(1)}, u32[]{:S(2)}, u32[]{:S(2)}) collective-permute-start(bf16[32,4096]{1,0:T(8,128)(2,1)S(1)} %get-tuple-element.8.refs_0_), channel_id=1, source_target_pairs={{0,1},{1,2},{2,3},{3,4},{4,5},{5,6},{6,7},{7,0},{8,9},{9,10},{10,1... | collective-permute-start | bytes 786440 | tf_op jit(solution)/shard_map/ppermute | solution.py:40
  28.1 10.2 %collective-permute-start.2 = (bf16[32,4096]{1,0:T(8,128)(2,1)S(1)}, bf16[32,4096]{1,0:T(8,128)(2,1)S(1)}, u32[]{:S(2)}, u32[]{:S(2)}) collective-permute-start(bf16[32,4096]{1,0:T(8,128)(2,1)S(1)} %collective-permute-done.1.refs_1_), channel_id=1, source_target_pairs={{0,7},{1,0},{2,1},{3,2},{4,3},{5,4},{6,5},{7,6},{8,15},{9,8},{10,9... | collective-permute-start | bytes 786440 | tf_op jit(solution)/shard_map/ppermute | solution.py:40
  32.1 10.3 %collective-permute-start.5 = (bf16[32,4096]{1,0:T(8,128)(2,1)S(1)}, bf16[32,4096]{1,0:T(8,128)(2,1)}, u32[]{:S(2)}, u32[]{:S(2)}) collective-permute-start(bf16[32,4096]{1,0:T(8,128)(2,1)S(1)} %collective-permute-done.4.refs_7_), channel_id=1, source_target_pairs={{0,1},{1,2},{2,3},{3,4},{4,5},{5,6},{6,7},{7,0},{8,9},{9,10},{10,1... | collective-permute-start | bytes 786440 | tf_op jit(solution)/shard_map/ppermute | solution.py:40
  38.3 21.5 %copy-start.7 = (bf16[32,4096]{1,0:T(8,128)(2,1)}, bf16[32,4096]{1,0:T(8,128)(2,1)S(1)}, u32[]{:S(2)}) copy-start(bf16[32,4096]{1,0:T(8,128)(2,1)S(1)} %collective-permute-done.2.refs_2_) | copy-start | bytes 786436
  38.3 9.0 %collective-permute-start.3 = (bf16[32,4096]{1,0:T(8,128)(2,1)S(1)}, bf16[32,4096]{1,0:T(8,128)(2,1)S(1)}, u32[]{:S(2)}, u32[]{:S(2)}) collective-permute-start(bf16[32,4096]{1,0:T(8,128)(2,1)S(1)} %collective-permute-done.2.refs_2_), channel_id=1, source_target_pairs={{0,7},{1,0},{2,1},{3,2},{4,3},{5,4},{6,5},{7,6},{8,15},{9,8},{10,9... | collective-permute-start | bytes 786440 | tf_op jit(solution)/shard_map/ppermute | solution.py:40
  42.4 9.2 %collective-permute-start.6 = (bf16[32,4096]{1,0:T(8,128)(2,1)}, bf16[32,4096]{1,0:T(8,128)(2,1)S(1)}, u32[]{:S(2)}, u32[]{:S(2)}) collective-permute-start(bf16[32,4096]{1,0:T(8,128)(2,1)} %collective-permute-done.5.refs_6_), channel_id=1, source_target_pairs={{0,1},{1,2},{2,3},{3,4},{4,5},{5,6},{6,7},{7,0},{8,9},{9,10},{10,1... | collective-permute-start | bytes 786440 | tf_op jit(solution)/shard_map/ppermute | solution.py:40
  48.0 6.8 %collective-permute-start.8 = (bf16[16,4096]{1,0:T(8,128)(2,1)}, bf16[16,4096]{1,0:T(8,128)(2,1)}, u32[]{:S(2)}, u32[]{:S(2)}) collective-permute-start(bf16[16,4096]{1,0:T(8,128)(2,1)} %slice.94), channel_id=1, source_target_pairs={{0,7},{1,0},{2,1},{3,2},{4,3},{5,4},{6,5},{7,6},{8,15},{9,8},{10,9... | collective-permute-start | bytes 393224 | tf_op jit(solution)/shard_map/ppermute | solution.py:40
  52.3 6.5 %collective-permute-start.7 = (bf16[16,4096]{1,0:T(8,128)(2,1)}, bf16[16,4096]{1,0:T(8,128)(2,1)}, u32[]{:S(2)}, u32[]{:S(2)}) collective-permute-start(bf16[16,4096]{1,0:T(8,128)(2,1)} %slice.93), channel_id=1, source_target_pairs={{0,1},{1,2},{2,3},{3,4},{4,5},{5,6},{6,7},{7,0},{8,9},{9,10},{10,1... | collective-permute-start | bytes 393224 | tf_op jit(solution)/shard_map/ppermute | solution.py:40
  59.9 2.2 %copy-start = (bf16[4096,512]{1,0:T(8,128)(2,1)S(1)}, bf16[4096,512]{1,0:T(8,128)(2,1)}, u32[]{:S(2)}) copy-start(bf16[4096,512]{1,0:T(8,128)(2,1)} %refs_10_.1) | copy-start | bytes 12582916
  62.0 0.9 copy-start.6
  63.0 0.9 copy-start.8
  69.0 4.5 %copy-start.10 = (s32[1,2,1024]{2,1,0:T(2,128)S(1)}, s32[1,2,1024]{2,1,0:T(2,128)}, u32[]{:S(2)}) copy-start(s32[1,2,1024]{2,1,0:T(2,128)} %param.18) | copy-start | bytes 24580
  73.3 56.4 %collective-permute-start.10 = (bf16[256,8,256]{2,1,0:T(8,128)(2,1)}, bf16[256,8,256]{2,1,0:T(8,128)(2,1)S(1)}, u32[]{:S(2)}, u32[]{:S(2)}) collective-permute-start(bf16[256,8,256]{2,1,0:T(8,128)(2,1)} %get-tuple-element.14), channel_id=1, source_target_pairs={{0,8},{8,16},{16,24},{24,32},{32,40},{40,48},{48,56},{56,64},{64,7... | collective-permute-start | bytes 3145736 | tf_op jit(solution)/shard_map/ppermute | solution.py:40
  73.3 56.4 %collective-permute-start.11 = (bf16[256,8,256]{2,1,0:T(8,128)(2,1)}, bf16[256,8,256]{2,1,0:T(8,128)(2,1)S(1)}, u32[]{:S(2)}, u32[]{:S(2)}) collective-permute-start(bf16[256,8,256]{2,1,0:T(8,128)(2,1)} %get-tuple-element.13), channel_id=1, source_target_pairs={{0,8},{8,16},{16,24},{24,32},{32,40},{40,48},{48,56},{56,64},{64,7... | collective-permute-start | bytes 3145736 | tf_op jit(solution)/shard_map/ppermute | solution.py:40
  73.3 56.4 %collective-permute-start.12 = (bf16[256,8,256]{2,1,0:T(8,128)(2,1)}, bf16[256,8,256]{2,1,0:T(8,128)(2,1)S(1)}, u32[]{:S(2)}, u32[]{:S(2)}) collective-permute-start(bf16[256,8,256]{2,1,0:T(8,128)(2,1)} %get-tuple-element.15), channel_id=1, source_target_pairs={{0,8},{8,16},{16,24},{24,32},{32,40},{40,48},{48,56},{56,64},{64,7... | collective-permute-start | bytes 3145736 | tf_op jit(solution)/shard_map/ppermute | solution.py:40
  73.4 56.3 %collective-permute-start.13 = (bf16[256,8,256]{2,1,0:T(8,128)(2,1)}, bf16[256,8,256]{2,1,0:T(8,128)(2,1)}, u32[]{:S(2)}, u32[]{:S(2)}) collective-permute-start(bf16[256,8,256]{2,1,0:T(8,128)(2,1)} %get-tuple-element.12), channel_id=1, source_target_pairs={{0,8},{8,16},{16,24},{24,32},{32,40},{40,48},{48,56},{56,64},{64,7... | collective-permute-start | bytes 3145736 | tf_op jit(solution)/shard_map/ppermute | solution.py:40
  73.5 53.3 %collective-permute-start.9 = (s32[1024]{0:T(1024)S(1)}, s32[1024]{0:T(1024)S(1)}, u32[]{:S(2)}, u32[]{:S(2)}) collective-permute-start(s32[1024]{0:T(1024)S(1)} %bitcast.26), channel_id=1, source_target_pairs={{0,8},{8,16},{16,24},{24,32},{32,40},{40,48},{48,56},{56,64},{64,7... | collective-permute-start | bytes 12296 | tf_op jit(solution)/shard_map/ppermute | solution.py:40
  140.9 7.6 %collective-permute-start.14 = (bf16[32,2048]{1,0:T(8,128)(2,1)S(1)}, bf16[32,2048]{1,0:T(8,128)(2,1)S(1)}, u32[]{:S(2)}, u32[]{:S(2)}) collective-permute-start(bf16[32,2048]{1,0:T(8,128)(2,1)S(1)} %get-tuple-element.20), channel_id=1, source_target_pairs={{0,1},{1,2},{2,3},{3,4},{4,5},{5,6},{6,7},{7,0},{8,9},{9,10},{10,1... | collective-permute-start | bytes 393224 | tf_op jit(solution)/shard_map/ppermute | solution.py:40
  141.0 7.5 %collective-permute-start.18 = (bf16[32,2048]{1,0:T(8,128)(2,1)S(1)}, bf16[32,2048]{1,0:T(8,128)(2,1)S(1)}, u32[]{:S(2)}, u32[]{:S(2)}) collective-permute-start(bf16[32,2048]{1,0:T(8,128)(2,1)S(1)} %get-tuple-element.21), channel_id=1, source_target_pairs={{0,7},{1,0},{2,1},{3,2},{4,3},{5,4},{6,5},{7,6},{8,15},{9,8},{10,9... | collective-permute-start | bytes 393224 | tf_op jit(solution)/shard_map/ppermute | solution.py:40
  148.6 7.7 %collective-permute-start.15 = (bf16[32,4096]{1,0:T(8,128)(2,1)S(1)}, bf16[32,4096]{1,0:T(8,128)(2,1)S(1)}, u32[]{:S(2)}, u32[]{:S(2)}) collective-permute-start(bf16[32,4096]{1,0:T(8,128)(2,1)S(1)} %pad_maximum_fusion.1), channel_id=1, source_target_pairs={{0,1},{1,2},{2,3},{3,4},{4,5},{5,6},{6,7},{7,0},{8,9},{9,10},{10,1... | collective-permute-start | bytes 786440 | tf_op jit(solution)/shard_map/ppermute | solution.py:40
  148.7 19.0 %collective-permute-start.19 = (bf16[32,4096]{1,0:T(8,128)(2,1)S(1)}, bf16[32,4096]{1,0:T(8,128)(2,1)S(1)}, u32[]{:S(2)}, u32[]{:S(2)}) collective-permute-start(bf16[32,4096]{1,0:T(8,128)(2,1)S(1)} %pad_maximum_fusion.2), channel_id=1, source_target_pairs={{0,7},{1,0},{2,1},{3,2},{4,3},{5,4},{6,5},{7,6},{8,15},{9,8},{10,9... | collective-permute-start | bytes 786440 | tf_op jit(solution)/shard_map/ppermute | solution.py:40
  156.3 22.6 %copy-start.9 = (s32[32,32]{1,0:T(8,128)S(1)}, s32[32,32]{1,0:T(8,128)}, u32[]{:S(2)}) copy-start(s32[32,32]{1,0:T(8,128)} %param.21) | copy-start | bytes 12292
  156.3 26.5 %copy-start.4 = (bf16[32,4096]{1,0:T(8,128)(2,1)S(1)}, bf16[32,4096]{1,0:T(8,128)(2,1)}, u32[]{:S(2)}) copy-start(bf16[32,4096]{1,0:T(8,128)(2,1)} %copy-done.3) | copy-start | bytes 786436
  156.3 11.4 %collective-permute-start.16 = (bf16[32,4096]{1,0:T(8,128)(2,1)S(1)}, bf16[32,4096]{1,0:T(8,128)(2,1)S(1)}, u32[]{:S(2)}, u32[]{:S(2)}) collective-permute-start(bf16[32,4096]{1,0:T(8,128)(2,1)S(1)} %add_convert_fusion.4), channel_id=1, source_target_pairs={{0,1},{1,2},{2,3},{3,4},{4,5},{5,6},{6,7},{7,0},{8,9},{9,10},{10,1... | collective-permute-start | bytes 786440 | tf_op jit(solution)/shard_map/ppermute | solution.py:40
  167.9 7.2 %collective-permute-start.20 = (bf16[32,4096]{1,0:T(8,128)(2,1)S(1)}, bf16[32,4096]{1,0:T(8,128)(2,1)S(1)}, u32[]{:S(2)}, u32[]{:S(2)}) collective-permute-start(bf16[32,4096]{1,0:T(8,128)(2,1)S(1)} %get-tuple-element.17), channel_id=1, source_target_pairs={{0,7},{1,0},{2,1},{3,2},{4,3},{5,4},{6,5},{7,6},{8,15},{9,8},{10,9... | collective-permute-start | bytes 786440 | tf_op jit(solution)/shard_map/ppermute | solution.py:40
  171.2 8.8 %collective-permute-start.17 = (bf16[32,4096]{1,0:T(8,128)(2,1)S(1)}, bf16[32,4096]{1,0:T(8,128)(2,1)S(1)}, u32[]{:S(2)}, u32[]{:S(2)}) collective-permute-start(bf16[32,4096]{1,0:T(8,128)(2,1)S(1)} %get-tuple-element.16), channel_id=1, source_target_pairs={{0,1},{1,2},{2,3},{3,4},{4,5},{5,6},{6,7},{7,0},{8,9},{9,10},{10,1... | collective-permute-start | bytes 786440 | tf_op jit(solution)/shard_map/ppermute | solution.py:40
  175.1 7.7 %collective-permute-start.21 = (bf16[32,4096]{1,0:T(8,128)(2,1)S(1)}, bf16[32,4096]{1,0:T(8,128)(2,1)S(1)}, u32[]{:S(2)}, u32[]{:S(2)}) collective-permute-start(bf16[32,4096]{1,0:T(8,128)(2,1)S(1)} %add_convert_fusion.1), channel_id=1, source_target_pairs={{0,7},{1,0},{2,1},{3,2},{4,3},{5,4},{6,5},{7,6},{8,15},{9,8},{10,9... | collective-permute-start | bytes 786440 | tf_op jit(solution)/shard_map/ppermute | solution.py:40
  (2 other events, 1.4 us)
Sparse Core Ops, SparseCore 0:
  69.1 76.7 all-gather.1
